TPU v7x, 32 devices: a whole 2x2x4 slice. The times are simulated.
32 devices in a mesh: pipe: 8 (over z, y), tensor: 4 (over x, core).
Axes of the slice: x: 2, y: 2, z: 4, core: 2. Of those that a mesh axis runs over, the one named last changes fastest.
Arguments:
- residual: bfloat16 [8, 128, 4096], P('pipe'), may hold values from -4 to 4
- out_proj: bfloat16 [8, 4096, 4096], P('pipe', 'tensor'), may hold values from -0.25 to 0.25
- attn_in: bfloat16 [8, 3, 128, 4096], P('pipe', None, None, 'tensor'), may hold values from -9 to 9
- stash_slots: bfloat16 [8, 2, 3, 128, 4096], P('pipe', None, None, None, 'tensor'), may hold values from -9 to 9
- grad_in: bfloat16 [8, 128, 4096], P('pipe'), may hold values from -6 to 6
- stash_slot: int32 [8], replicated, may hold values from 0 to 1
Outputs:
- fwd_out: bfloat16 [8, 128, 4096], P('pipe')
- qkv_grad: bfloat16 [8, 3, 128, 4096], P('pipe', None, None, 'tensor')
- evicted: bfloat16 [8, 3, 128, 4096], P('pipe', None, None, 'tensor')
All inputs are finite; a program needn't handle non-finite values.
Results may differ from a plain program's by a relative error of at most 0.0065.
Values may be sent and summed in bfloat16 or wider, within the bound.
A program may use at most 64 MiB of HBM per device.

v0:
```python
import jax
import jax.numpy as jnp
from jax import lax
from jax.sharding import PartitionSpec as P

HD = 128


def shifted(block, axis, distance):
    devices = range(lax.axis_size(axis))
    route = [((i - distance) % len(devices), i) for i in devices]
    return lax.ppermute(block, axis, route)


def head_probs(query_in, key_in):
    length = query_in.shape[0]
    query_heads = query_in.astype(jnp.float32).reshape(length, -1, HD)
    key_heads = key_in.astype(jnp.float32).reshape(length, -1, HD)
    scores = jnp.einsum("ihd,jhd->hij", query_heads, key_heads) * HD ** (-0.5)
    row_ids = jnp.arange(length, dtype=jnp.int32)
    allowed = row_ids[:, None] >= row_ids[None, :]
    scores = jnp.where(allowed[None], scores, -jnp.inf)
    return jax.nn.softmax(scores, axis=-1)


def attend(inputs):
    length = inputs.shape[1]
    attn_probs = head_probs(inputs[0], inputs[1])
    probs_low = lax.optimization_barrier(attn_probs.astype(jnp.bfloat16)).astype(jnp.float32)
    value_heads = inputs[2].astype(jnp.float32).reshape(length, -1, HD)
    context = jnp.einsum("hij,jhd->ihd", probs_low, value_heads)
    return context.reshape(length, -1).astype(jnp.bfloat16)


def attend_back(stored, grad_context):
    length = stored.shape[1]
    scale_factor = HD ** (-0.5)
    attn_probs = head_probs(stored[0], stored[1])
    grad_heads = lax.optimization_barrier(grad_context).astype(jnp.float32).reshape(length, -1, HD)
    query_heads = stored[0].astype(jnp.float32).reshape(length, -1, HD)
    key_heads = stored[1].astype(jnp.float32).reshape(length, -1, HD)
    value_heads = stored[2].astype(jnp.float32).reshape(length, -1, HD)
    grad_probs = jnp.einsum("ihd,jhd->hij", grad_heads, value_heads)
    row_delta = jnp.sum(attn_probs * grad_probs, axis=-1, keepdims=True)
    grad_scores = (attn_probs * (grad_probs - row_delta)).astype(jnp.bfloat16)
    grad_scores = lax.optimization_barrier(grad_scores).astype(jnp.float32)
    probs_low = lax.optimization_barrier(attn_probs.astype(jnp.bfloat16)).astype(jnp.float32)
    grad_query = jnp.einsum("hij,jhd->ihd", grad_scores, key_heads) * scale_factor
    grad_key = jnp.einsum("hij,ihd->jhd", grad_scores, query_heads) * scale_factor
    grad_value = jnp.einsum("hij,ihd->jhd", probs_low, grad_heads)
    stacked = jnp.stack([grad_query, grad_key, grad_value], axis=0)
    return stacked.reshape(3, length, -1).astype(jnp.bfloat16)


def on_device(residual, out_proj, attn_in, stash_slots, grad_in, stash_slot):
    sections = lax.axis_size("pipe")
    half_way = sections // 2
    own_section = lax.axis_index("pipe")
    partner = (own_section + half_way) % sections
    wanted_slot = lax.dynamic_index_in_dim(stash_slot, partner, 0, keepdims=False)
    request = lax.dynamic_index_in_dim(stash_slots[0], wanted_slot, 0, keepdims=False)
    weight = out_proj[0]
    evicted, stored = shifted((attn_in[0], request), "pipe", half_way)
    context = attend(attn_in[0])
    branch = jnp.dot(context, weight, preferred_element_type=jnp.float32)
    summed = lax.psum(branch, "tensor")
    section_out = (residual[0].astype(jnp.float32) + summed).astype(jnp.bfloat16)
    arrived = shifted(section_out, "pipe", 1)
    fwd_out = arrived[None]
    grad_context = lax.dot_general(
        grad_in[0], weight, (((1,), (1,)), ((), ())), preferred_element_type=jnp.float32
    )
    qkv_grad = attend_back(stored, grad_context.astype(jnp.bfloat16))[None]
    return (fwd_out, qkv_grad, evicted[None])


def solution(mesh):
    in_specs = (
        P("pipe", None, None),
        P("pipe", "tensor", None),
        P("pipe", None, None, "tensor"),
        P("pipe", None, None, None, "tensor"),
        P("pipe", None, None),
        P(),
    )
    out_specs = (
        P("pipe", None, None),
        P("pipe", None, None, "tensor"),
        P("pipe", None, None, "tensor"),
    )
    return jax.shard_map(
        on_device, mesh=mesh, in_specs=in_specs, out_specs=out_specs, check_vma=False
    )
```

profile of v0, /device:TPU:17, one launch (start us, length us, event | category | flops | bytes accessed | tf_op | source)
XLA Modules:
  0.0 117.7 jit_solution(1240197204988377578)
XLA Ops:
  7.2 0.0 copy-start
  7.2 0.0 all-reduce.2.cloned.1.call-start
  7.2 1.3 %dynamic_slice.8 = s32[1]{0:T(128)} dynamic-slice(s32[8]{0:T(128)} %param.11, s32[]{:T(128)S(6)} %select_n.24), dynamic_slice_sizes={1} | dynamic-slice | bytes 12 | tf_op jit(solution)/shard_map/jit(dynamic_index_in_dim)/dynamic_slice | solution.py:60
  10.5 0.0 copy-done
  10.5 0.1 constant_dynamic-slice_fusion
  10.6 1.2 copy.27
  11.8 0.0 collective-permute-start.1
  11.8 1.2 fusion.28
  13.0 0.2 copy.25
  13.1 0.2 copy.52
  13.3 0.2 copy.53
  13.5 0.4 fusion.29
  13.9 0.1 divide_convert_fusion
  13.9 0.2 convolution_convert_fusion
  14.2 6.0 %fusion.5 = f32[128,4096]{1,0:T(8,128)} fusion(bf16[128,1024]{0,1:T(8,128)(2,1)S(1)} %bitcast.54, bf16[1,1024,4096]{2,1,0:T(8,128)(2,1)} %param.7), kind=kOutput, calls=%fused_computation.5 | convolution fusion | flops 1073741824 | bytes 10747904 | tf_op jit(solution)/shard_map/dot_general | solution.py:65
  20.1 0.0 copy-start.1
  20.1 0.0 all-reduce.2.cloned.1.call-update
  20.2 2.4 %collective-permute-start.2 = (bf16[3,128,1024]{2,1,0:T(8,128)(2,1)}, bf16[3,128,1024]{2,1,0:T(8,128)(2,1)}, u32[]{:S(2)}, u32[]{:S(2)}) collective-permute-start(bf16[3,128,1024]{2,1,0:T(8,128)(2,1)} %bitcast.20), channel_id=1, source_target_pairs={{16,0},{20,4},{24,8},{28,12},{0,16},{4,20},{8,24},{12,28},{17,1},{... | collective-permute-start | bytes 2359304 | tf_op jit(solution)/shard_map/ppermute | solution.py:12
  22.6 0.0 copy-done.1
  22.6 6.3 %fusion.17 = bf16[128,1024]{1,0:T(8,128)(2,1)S(1)} fusion(bf16[1,1024,4096]{2,1,0:T(8,128)(2,1)} %param.7, bf16[1,128,4096]{2,1,0:T(8,128)(2,1)S(1)} %copy-done.1), kind=kOutput, calls=%fused_computation.22 | convolution fusion | flops 1073872896 | bytes 9699328 | tf_op jit(solution)/shard_map/dot_general | solution.py:70
  28.9 0.2 copy.54
  29.0 33.3 %collective-permute-done.1 = bf16[3,128,1024]{1,2,0:T(8,128)(2,1)} collective-permute-done((bf16[3,128,1024]{1,2,0:T(8,128)(2,1)}, bf16[3,128,1024]{1,2,0:T(8,128)(2,1)}, u32[]{:S(2)}, u32[]{:S(2)}) %collective-permute-start.1) | collective-permute-done | bytes 786464 | tf_op jit(solution)/shard_map/ppermute | solution.py:12
  62.3 1.9 %fusion.27 = (bf16[1,128,1024]{1,2,0:T(8,128)(2,1)}, bf16[1,128,1024]{1,2,0:T(8,128)(2,1)S(1)}, bf16[1,128,1024]{1,2,0:T(8,128)(2,1)S(1)}) fusion(bf16[3,128,1024]{1,2,0:T(8,128)(2,1)} %collective-permute-done.1), kind=kLoop, calls=%fused_computation.38 | loop fusion | bytes 1572864 | tf_op jit(solution)/shard_map/slice | solution.py:42
  64.2 0.4 fusion.30
  64.6 0.1 fusion.26
  64.6 8.6 %all-reduce.2.cloned.1.call-done = f32[128,4096]{1,0:T(8,128)} async-done(((f32[128,4096]{1,0:T(8,128)}), f32[128,4096]{1,0:T(8,128)}) %all-reduce.2.cloned.1.call-update) | async-done | bytes 2097168 | tf_op jit(solution)/shard_map/psum | solution.py:66
  73.2 3.0 %fusion.7 = bf16[128,4096]{1,0:T(8,128)(2,1)} fusion(f32[128,4096]{1,0:T(8,128)} %all-reduce.2.cloned.1.call-done, bf16[1,128,4096]{2,1,0:T(8,128)(2,1)} %param.6), kind=kLoop, calls=%fused_computation.8 | loop fusion | flops 1572864 | bytes 4194304 | tf_op jit(solution)/shard_map/convert_element_type | solution.py:67
  76.3 1.2 %collective-permute-start = (bf16[128,4096]{1,0:T(8,128)(2,1)}, bf16[128,4096]{1,0:T(8,128)(2,1)}, u32[]{:S(2)}, u32[]{:S(2)}) collective-permute-start(bf16[128,4096]{1,0:T(8,128)(2,1)} %fusion.7), channel_id=1, source_target_pairs={{28,0},{0,4},{4,8},{8,12},{12,16},{16,20},{20,24},{24,28},{29,1},{... | collective-permute-start | bytes 3145736 | tf_op jit(solution)/shard_map/ppermute | solution.py:12
  77.5 1.4 %fusion.16 = bf16[8,128,128]{1,2,0:T(8,128)(2,1)S(1)} fusion(f32[8,128,128]{1,2,0:T(8,128)S(1)} %get-tuple-element.15, f32[8,128]{1,0:T(8,128)S(1)} %get-tuple-element.14, bf16[128,8,128]{0,2,1:T(8,128)(2,1)S(1)} %bitcast.55, bf16[128,8,128]{0,2,1:T(8,128)(2,1)} %bitcast.67), kind=kOutput, calls=%fused_computation.21 | convolution fusion | flops 67896448 | bytes 1314816 | tf_op jit(solution)/shard_map/sub | solution.py:45
  78.9 0.3 fusion.22
  79.2 0.2 copy.37
  79.4 0.3 fusion.23
  79.7 0.2 copy.34
  79.9 0.3 convolution_convert_fusion.1
  80.2 0.1 pad_maximum_fusion
  80.3 1.2 copy.40
  81.5 0.0 collective-permute-done.2
  81.5 25.0 %collective-permute-done = bf16[128,4096]{1,0:T(8,128)(2,1)} collective-permute-done((bf16[128,4096]{1,0:T(8,128)(2,1)}, bf16[128,4096]{1,0:T(8,128)(2,1)}, u32[]{:S(2)}, u32[]{:S(2)}) %collective-permute-start) | collective-permute-done | bytes 1048608 | tf_op jit(solution)/shard_map/ppermute | solution.py:12
  106.5 2.3 %copy.58 = bf16[1,128,4096]{2,1,0:T(8,128)(2,1)} copy(bf16[1,128,4096]{2,1,0:T(8,128)(2,1)} %bitcast.7) | data formatting | bytes 2097152
  108.8 2.1 %copy.59 = bf16[1,3,128,1024]{3,2,1,0:T(8,128)(2,1)} copy(bf16[1,3,128,1024]{3,2,1,0:T(8,128)(2,1)} %bitcast.21) | data formatting | bytes 1572864
  (1 shorter events, 0.0 us)
Async XLA Ops:
  7.2 3.4 %copy-start = (bf16[1,2,3,128,1024]{4,3,2,1,0:T(8,128)(2,1)S(1)}, bf16[1,2,3,128,1024]{4,3,2,1,0:T(8,128)(2,1)}, u32[]{:S(2)}) copy-start(bf16[1,2,3,128,1024]{4,3,2,1,0:T(8,128)(2,1)} %param.9) | copy-start | bytes 4718596
  7.2 66.1 %all-reduce.2.cloned.1.call-start = ((), (), s32[]{:S(2)}) async-start(), calls=%async_computation | async-start | bytes 4194304 | tf_op jit(solution)/shard_map/psum | solution.py:66
  11.8 50.6 %collective-permute-start.1 = (bf16[3,128,1024]{1,2,0:T(8,128)(2,1)}, bf16[3,128,1024]{1,2,0:T(8,128)(2,1)}, u32[]{:S(2)}, u32[]{:S(2)}) collective-permute-start(bf16[3,128,1024]{1,2,0:T(8,128)(2,1)} %bitcast.9), channel_id=1, source_target_pairs={{16,0},{20,4},{24,8},{28,12},{0,16},{4,20},{8,24},{12,28},{17,1},{... | collective-permute-start | bytes 2359304 | tf_op jit(solution)/shard_map/ppermute | solution.py:12
  20.1 2.5 %copy-start.1 = (bf16[1,128,4096]{2,1,0:T(8,128)(2,1)S(1)}, bf16[1,128,4096]{2,1,0:T(8,128)(2,1)}, u32[]{:S(2)}) copy-start(bf16[1,128,4096]{2,1,0:T(8,128)(2,1)} %param.10) | copy-start | bytes 3145732
  20.2 61.3 %collective-permute-start.2 = (bf16[3,128,1024]{2,1,0:T(8,128)(2,1)}, bf16[3,128,1024]{2,1,0:T(8,128)(2,1)}, u32[]{:S(2)}, u32[]{:S(2)}) collective-permute-start(bf16[3,128,1024]{2,1,0:T(8,128)(2,1)} %bitcast.20), channel_id=1, source_target_pairs={{16,0},{20,4},{24,8},{28,12},{0,16},{4,20},{8,24},{12,28},{17,1},{... | collective-permute-start | bytes 2359304 | tf_op jit(solution)/shard_map/ppermute | solution.py:12
  76.3 30.2 %collective-permute-start = (bf16[128,4096]{1,0:T(8,128)(2,1)}, bf16[128,4096]{1,0:T(8,128)(2,1)}, u32[]{:S(2)}, u32[]{:S(2)}) collective-permute-start(bf16[128,4096]{1,0:T(8,128)(2,1)} %fusion.7), channel_id=1, source_target_pairs={{28,0},{0,4},{4,8},{8,12},{12,16},{16,20},{20,24},{24,28},{29,1},{... | collective-permute-start | bytes 3145736 | tf_op jit(solution)/shard_map/ppermute | solution.py:12
Sparse Core Ops, SparseCore 0:
  20.3 52.9 all-reduce.1
where the time goes:
time: 118 us
  waiting for transfers between devices  66.9 us (57%)
  between operations  16.1 us (14%)
  matrix products  15.6 us (13%)
  local copies, waits for them, and re-layouts  12.2 us (10%)
  starting transfers between devices  3.66 us (3%)
  other arithmetic  3.25 us (3%)
    ppermute x3, waiting for transfers between devices, shifted(): return lax.ppermute(block, axis, route)  58.3 us
    psum x1, waiting for transfers between devices, on_device(): summed = lax.psum(branch, 'tensor')  8.62 us
    dot_general x1, matrix products, on_device(): lax.dot_general(grad_in[0], weight, (((1,), (1,)), ((), ())), preferred_e...  6.26 us
    dot_general x1, matrix products, on_device(): branch = jnp.dot(context, weight, preferred_element_type=jnp.float32)  5.97 us
    unnamed x9, local copies, waits for them, and re-layouts  5.87 us
    ppermute x3, starting transfers between devices, shifted(): return lax.ppermute(block, axis, route)  3.62 us
    convert_element_type x1, other arithmetic, on_device(): (residual[0].astype(jnp.float32) + summed).astype(jnp.bfloat16)  3.04 us
  transfers between devices with their start and end apart: 4, of which 3 were waited for; matrix products, arithmetic and copies ran while one was open for 20% of the time, Pallas kernels for 0%

commit v1 on v0

v1 whole, which is shorter than its diff:
```python
import functools

import jax
import jax.numpy as jnp
from jax import lax
from jax.experimental import pallas as pl
from jax.experimental.pallas import tpu as pltpu
from jax.sharding import PartitionSpec as P

HD = 128
MESH = pl.DeviceIdType.MESH
VMEM_LIMIT = 40 * 1024 * 1024
ACROSS = (((1,), (1,)), ((), ()))
DOWN = (((0,), (0,)), ((), ()))


def mult(a, b, dims):
    return lax.dot_general(a, b, dims, preferred_element_type=jnp.float32)


def head_probs(query, key):
    length = query.shape[0]
    scores = mult(query, key, ACROSS) * HD ** (-0.5)
    row_ids = lax.broadcasted_iota(jnp.int32, (length, length), 0)
    col_ids = lax.broadcasted_iota(jnp.int32, (length, length), 1)
    scores = jnp.where(row_ids >= col_ids, scores, -jnp.inf)
    top = jnp.max(scores, axis=-1, keepdims=True)
    raised = jnp.exp(scores - top)
    return raised / jnp.sum(raised, axis=-1, keepdims=True)


def tick(
    sections,
    group,
    slot_ref,
    residual_ref,
    weight_ref,
    attn_ref,
    stash_ref,
    grad_ref,
    fwd_ref,
    qkv_ref,
    evict_ref,
    weight,
    attn,
    stash,
    grad,
    resid,
    request,
    stored,
    context,
    grad_context,
    own_sum,
    sums_out,
    sums_in,
    piece_out,
    piece_in,
    qkv,
    local_sem,
    evict_send,
    evict_recv,
    request_send,
    request_recv,
    sums_send,
    sums_recv,
    piece_send,
    piece_recv,
    gather_send,
    gather_recv,
):
    section = lax.axis_index("pipe")
    shard = lax.axis_index("tensor")
    partner = lax.rem(section + sections // 2, sections)
    following = lax.rem(section + 1, sections)
    before = lax.rem(section + sections - 1, sections)
    parts, rows, local = attn.shape
    width = piece_out.shape[1]
    heads = local // HD

    def peer(distance):
        return lax.rem(shard + distance, group)

    def lanes(index, size):
        return pl.ds(pl.multiple_of(index * size, size), size)

    loads = []
    for number, (source, target) in enumerate(
        (
            (stash_ref.at[0], stash),
            (attn_ref.at[0], attn),
            (weight_ref.at[0], weight),
            (grad_ref.at[0], grad),
            (residual_ref.at[0, :, lanes(shard, width)], resid),
        )
    ):
        load = pltpu.make_async_copy(source, target, local_sem.at[number])
        load.start()
        loads.append(load)

    barrier = pltpu.get_barrier_semaphore()
    for other in (partner, following, before):
        pl.semaphore_signal(barrier, inc=1, device_id=(other, shard), device_id_type=MESH)
    for distance in range(1, group):
        pl.semaphore_signal(
            barrier, inc=1, device_id=(section, peer(distance)), device_id_type=MESH
        )
    pl.semaphore_wait(barrier, 3 + group - 1)

    evictions = [
        pltpu.make_async_remote_copy(
            src_ref=attn_ref.at[0, part],
            dst_ref=evict_ref.at[0, part],
            send_sem=evict_send.at[part],
            recv_sem=evict_recv.at[part],
            device_id=(partner, shard),
            device_id_type=MESH,
        )
        for part in range(parts)
    ]
    requests = [
        pltpu.make_async_remote_copy(
            src_ref=request.at[part],
            dst_ref=stored.at[part],
            send_sem=request_send.at[part],
            recv_sem=request_recv.at[part],
            device_id=(partner, shard),
            device_id_type=MESH,
        )
        for part in range(parts)
    ]

    evictions[0].start()
    wanted = slot_ref[partner]
    loads[0].wait()
    for part in range(parts):
        request[part] = stash[wanted, part]
        requests[part].start()

    loads[1].wait()

    def attend(head, _):
        cols = lanes(head, HD)
        probs = head_probs(attn[0, :, cols], attn[1, :, cols]).astype(jnp.bfloat16)
        values = attn[2, :, cols]
        context[:, cols] = jnp.dot(
            probs, values, preferred_element_type=jnp.float32
        ).astype(jnp.bfloat16)
        return 0

    lax.fori_loop(0, heads, attend, 0, unroll=2)

    loads[2].wait()
    transfers = []
    for distance in range(1, group):
        target = peer(distance)
        sums_out[distance - 1] = jnp.dot(
            context[...], weight[:, lanes(target, width)], preferred_element_type=jnp.float32
        )
        transfer = pltpu.make_async_remote_copy(
            src_ref=sums_out.at[distance - 1],
            dst_ref=sums_in.at[distance - 1],
            send_sem=sums_send.at[distance - 1],
            recv_sem=sums_recv.at[distance - 1],
            device_id=(section, target),
            device_id_type=MESH,
        )
        transfer.start()
        transfers.append(transfer)
    loads[4].wait()
    own_sum[...] = resid[...].astype(jnp.float32) + jnp.dot(
        context[...], weight[:, lanes(shard, width)], preferred_element_type=jnp.float32
    )

    loads[3].wait()
    tile = min(local, 2 * HD)

    def back_project(step, _):
        cols = lanes(step, tile)
        grad_context[:, cols] = mult(grad[...], weight[cols, :], ACROSS).astype(jnp.bfloat16)
        return 0

    lax.fori_loop(0, local // tile, back_project, 0)

    for transfer in transfers:
        transfer.wait()
    total = own_sum[...]
    for distance in range(1, group):
        total = total + sums_in[distance - 1]
    piece_out[...] = total.astype(jnp.bfloat16)
    hand_over = pltpu.make_async_remote_copy(
        src_ref=piece_out,
        dst_ref=piece_in,
        send_sem=piece_send.at[0],
        recv_sem=piece_recv.at[0],
        device_id=(following, shard),
        device_id_type=MESH,
    )
    hand_over.start()
    for part in range(1, parts):
        evictions[part].start()

    hand_over.wait()
    own_columns = lanes(shard, width)
    gathers = []
    for distance in range(1, group):
        gather = pltpu.make_async_remote_copy(
            src_ref=piece_in,
            dst_ref=fwd_ref.at[0, :, own_columns],
            send_sem=gather_send.at[distance - 1],
            recv_sem=gather_recv.at[distance - 1],
            device_id=(section, peer(distance)),
            device_id_type=MESH,
        )
        gather.start()
        gathers.append(gather)
    keep = pltpu.make_async_copy(piece_in, fwd_ref.at[0, :, own_columns], local_sem.at[5])
    keep.start()

    for copy in requests:
        copy.wait()

    def attend_back(head, _):
        cols = lanes(head, HD)
        query, key, value = (stored[part, :, cols] for part in range(3))
        grads = grad_context[:, cols]
        probs = head_probs(query, key)
        grad_probs = mult(grads, value, ACROSS)
        row_delta = jnp.sum(probs * grad_probs, axis=-1, keepdims=True)
        grad_scores = (probs * (grad_probs - row_delta)).astype(jnp.bfloat16)
        probs_low = probs.astype(jnp.bfloat16)
        grad_query = jnp.dot(grad_scores, key, preferred_element_type=jnp.float32)
        grad_key = mult(grad_scores, query, DOWN)
        qkv[0, :, cols] = (grad_query * HD ** (-0.5)).astype(jnp.bfloat16)
        qkv[1, :, cols] = (grad_key * HD ** (-0.5)).astype(jnp.bfloat16)
        qkv[2, :, cols] = mult(probs_low, grads, DOWN).astype(jnp.bfloat16)
        return 0

    lax.fori_loop(0, heads, attend_back, 0, unroll=2)
    put = pltpu.make_async_copy(qkv, qkv_ref.at[0], local_sem.at[6])
    put.start()

    keep.wait()
    put.wait()
    for copy in gathers:
        copy.wait()
    for copy in evictions:
        copy.wait()


def settle(*refs):
    count = (len(refs) - 1) // 2
    sources, targets, sem = refs[:count], refs[count : 2 * count], refs[-1]
    copies = []
    for number, (source, target) in enumerate(zip(sources, targets)):
        copy = pltpu.make_async_copy(source, target, sem.at[number])
        copy.start()
        copies.append(copy)
    for copy in copies:
        copy.wait()


def on_device(residual, out_proj, attn_in, stash_slots, grad_in, stash_slot):
    sections = lax.axis_size("pipe")
    group = lax.axis_size("tensor")
    _, parts, rows, local = attn_in.shape
    slots = stash_slots.shape[1]
    depth = residual.shape[2]
    width = depth // group
    anywhere = pl.BlockSpec(memory_space=pl.ANY)
    results = (
        jax.ShapeDtypeStruct((1, rows, depth), jnp.bfloat16),
        jax.ShapeDtypeStruct((1, parts, rows, local), jnp.bfloat16),
        jax.ShapeDtypeStruct((1, parts, rows, local), jnp.bfloat16),
    )
    low, full = jnp.bfloat16, jnp.float32
    flops = 4 * rows * local * depth + 16 * rows * rows * local
    made = pl.pallas_call(
        functools.partial(tick, sections, group),
        out_shape=results,
        in_specs=[pl.BlockSpec(memory_space=pltpu.SMEM)] + [anywhere] * 5,
        out_specs=(anywhere,) * 3,
        scratch_shapes=[
            pltpu.VMEM((local, depth), low),
            pltpu.VMEM((parts, rows, local), low),
            pltpu.VMEM((slots, parts, rows, local), low),
            pltpu.VMEM((rows, depth), low),
            pltpu.VMEM((rows, width), low),
            pltpu.VMEM((parts, rows, local), low),
            pltpu.VMEM((parts, rows, local), low),
            pltpu.VMEM((rows, local), low),
            pltpu.VMEM((rows, local), low),
            pltpu.VMEM((rows, width), full),
            pltpu.VMEM((group - 1, rows, width), full),
            pltpu.VMEM((group - 1, rows, width), full),
            pltpu.VMEM((rows, width), low),
            pltpu.VMEM((rows, width), low),
            pltpu.VMEM((parts, rows, local), low),
            pltpu.SemaphoreType.DMA((7,)),
            pltpu.SemaphoreType.DMA((parts,)),
            pltpu.SemaphoreType.DMA((parts,)),
            pltpu.SemaphoreType.DMA((parts,)),
            pltpu.SemaphoreType.DMA((parts,)),
            pltpu.SemaphoreType.DMA((group - 1,)),
            pltpu.SemaphoreType.DMA((group - 1,)),
            pltpu.SemaphoreType.DMA((1,)),
            pltpu.SemaphoreType.DMA((1,)),
            pltpu.SemaphoreType.DMA((group - 1,)),
            pltpu.SemaphoreType.DMA((group - 1,)),
        ],
        compiler_params=pltpu.CompilerParams(
            collective_id=0, has_side_effects=True, vmem_limit_bytes=VMEM_LIMIT
        ),
        cost_estimate=pl.CostEstimate(
            flops=flops, bytes_accessed=2 * local * depth, transcendentals=2 * rows * local
        ),
        name="tick",
    )(stash_slot, residual, out_proj, attn_in, stash_slots, grad_in)
    return pl.pallas_call(
        settle,
        out_shape=results,
        in_specs=[anywhere] * 3,
        out_specs=(anywhere,) * 3,
        scratch_shapes=[pltpu.SemaphoreType.DMA((3,))],
        name="settle",
    )(*made)


def solution(mesh):
    in_specs = (
        P("pipe", None, None),
        P("pipe", "tensor", None),
        P("pipe", None, None, "tensor"),
        P("pipe", None, None, None, "tensor"),
        P("pipe", None, None),
        P(),
    )
    out_specs = (
        P("pipe", None, None),
        P("pipe", None, None, "tensor"),
        P("pipe", None, None, "tensor"),
    )
    return jax.shard_map(
        on_device, mesh=mesh, in_specs=in_specs, out_specs=out_specs, check_vma=False
    )
```

time: 118 us -> 171 us (1.45)
  Pallas kernels: 0 us -> 161 us
  waiting for transfers between devices: 66.9 us -> 0 us
  matrix products: 15.6 us -> 0 us
  between operations: 16.1 us -> 0.66 us
  local copies, waits for them, and re-layouts: 12.2 us -> 8.4 us
  starting transfers between devices: 3.66 us -> 0 us
  other arithmetic: 3.25 us -> 0 us
    pallas_call x0 -> x2, Pallas kernels: none -> 161 us  [the longest x1 80.8 us: on_device(): pl.pallas_call(functools.partial(tick, sections, group), out_shape=result...]
    ppermute x3 -> x0, waiting for transfers between devices: 58.3 us -> none  [shifted(): return lax.ppermute(block, axis, route)]
    dot_general x6 -> x0, matrix products: 13.4 us -> none  [the longest x1 6.26 us: on_device(): lax.dot_general(grad_in[0], weight, (((1,), (1,)), ((), ())), preferred_e...]
    psum x1 -> x0, waiting for transfers between devices: 8.62 us -> none  [on_device(): summed = lax.psum(branch, 'tensor')]
    ppermute x3 -> x0, starting transfers between devices: 3.62 us -> none  [shifted(): return lax.ppermute(block, axis, route)]
    slice x3 -> x0, local copies, waits for them, and re-layouts: 3.2 us -> none  [the longest x1 1.87 us: attend_back(): value_heads = stored[2].astype(jnp.float32).reshape(length, -1, HD)]
    convert_element_type x3 -> x0, other arithmetic: 3.14 us -> none  [the longest x1 3.04 us: on_device(): (residual[0].astype(jnp.float32) + summed).astype(jnp.bfloat16)]
    dynamic_slice x3 -> x0, local copies, waits for them, and re-layouts: 2.56 us -> none  [the longest x1 1.35 us: on_device(): lax.dynamic_index_in_dim(stash_slot, partner, 0, keepdims=False)]
  transfers between devices with their start and end apart: 4 -> 0, of which waited for: 3 -> 0; matrix products, arithmetic and copies ran while one was open for 20% -> 0% of each run, Pallas kernels for 0% -> 0%
where the time goes in v1:
time: 171 us; the launch traced here: 170 us
  Pallas kernels  161 us (94%)
  local copies, waits for them, and re-layouts  8.4 us (5%)
    pallas_call x1, Pallas kernels, on_device(): pl.pallas_call(functools.partial(tick, sections, group), out_shape=result...  80.8 us
    pallas_call x1, Pallas kernels, on_device(): pl.pallas_call(settle, out_shape=results, in_specs=[anywhere] * 3, out_sp...  80.5 us
    unnamed x16, local copies, waits for them, and re-layouts  8.4 us

profile of v1, /device:TPU:17, one launch (start us, length us, event | category | flops | bytes accessed | tf_op | source)
XLA Modules:
  0.0 170.4 jit_solution(9413244499095318773)
XLA Ops:
  0.6 0.0 copy-start
  0.6 1.4 copy-done
  2.0 0.0 copy-start.1
  2.0 1.2 copy-done.1
  3.3 0.0 copy-start.2
  3.3 1.2 copy-done.2
  4.5 0.0 copy-start.4
  4.5 1.1 copy-done.4
  5.6 0.0 copy-start.7
  5.6 0.7 copy-done.7
  6.3 80.8 %tick.1 = (bf16[1,128,4096]{2,1,0:T(8,128)(2,1)S(1)}, bf16[1,3,128,1024]{3,2,1,0:T(8,128)(2,1)S(1)}, bf16[1,3,128,1024]{3,2,1,0:T(8,128)(2,1)S(1)}) custom-call(s32[8]{0:T(128)S(1)} %copy-done.7, bf16[1,128,4096]{2,1,0:T(8,128)(2,1)S(1)} %copy-done.1, bf16[1,1024,4096]{2,1,0:T(8,128)(2,1)} %weight_ref.1, bf16[1,3,128,1024]{3,2,1,0:T(8,128)(2,1)S(1)} %copy-done.4, ...), custom_call_target="tpu_custom_call" | custom-call | flops 2415919104 | bytes 8388608 | tf_op jit(solution)/shard_map/tick/pallas_call | solution.py:277
  87.1 0.0 copy-start.3
  87.1 1.0 copy-done.3
  88.1 0.0 copy-start.5
  88.1 0.9 copy-done.5
  89.0 0.0 copy-start.6
  89.0 0.9 copy-done.6
  89.9 80.5 %settle.1 = (bf16[1,128,4096]{2,1,0:T(8,128)(2,1)}, bf16[1,3,128,1024]{3,2,1,0:T(8,128)(2,1)}, bf16[1,3,128,1024]{3,2,1,0:T(8,128)(2,1)}) custom-call(bf16[1,128,4096]{2,1,0:T(8,128)(2,1)} %copy-done.3, bf16[1,3,128,1024]{3,2,1,0:T(8,128)(2,1)} %copy-done.5, bf16[1,3,128,1024]{3,2,1,0:T(8,128)(2,1)} %copy-done.6), custom_call_target="tpu_custom_call" | custom-call | tf_op jit(solution)/shard_map/settle/pallas_call | solution.py:318
Async XLA Ops:
  0.6 1.4 copy-start
  2.0 1.2 copy-start.1
  3.3 1.2 copy-start.2
  4.5 1.1 copy-start.4
  5.6 0.7 copy-start.7
  87.1 1.0 copy-start.3
  88.1 0.9 copy-start.5
  89.0 0.9 copy-start.6

commit v2 on v1

--- a/solution.py
+++ b/solution.py
@@ -9,7 +9,7 @@
 
 HD = 128
 MESH = pl.DeviceIdType.MESH
-VMEM_LIMIT = 40 * 1024 * 1024
+VMEM_LIMIT = 56 * 1024 * 1024
 ACROSS = (((1,), (1,)), ((), ()))
 DOWN = (((0,), (0,)), ((), ()))
 
@@ -248,15 +248,25 @@
 
 
 def settle(*refs):
-    count = (len(refs) - 1) // 2
-    sources, targets, sem = refs[:count], refs[count : 2 * count], refs[-1]
-    copies = []
-    for number, (source, target) in enumerate(zip(sources, targets)):
-        copy = pltpu.make_async_copy(source, target, sem.at[number])
-        copy.start()
-        copies.append(copy)
-    for copy in copies:
-        copy.wait()
+    count = (len(refs) - 2) // 3
+    sources, targets, staged = (refs[start * count : (start + 1) * count] for start in range(3))
+    sem_in, sem_out = refs[-2:]
+    loads, stores = [], []
+    for source, target, stage in zip(sources, targets, staged):
+        for part in range(stage.shape[0]):
+            number = len(loads)
+            size = stage.shape[1]
+            window = (0, pl.ds(part * size, size)) if len(source.shape) == 3 else (0, part)
+            here, there = source.at[window], target.at[window]
+            load = pltpu.make_async_copy(here, stage.at[part], sem_in.at[number])
+            load.start()
+            loads.append(load)
+            stores.append(pltpu.make_async_copy(stage.at[part], there, sem_out.at[number]))
+    for load, store in zip(loads, stores):
+        load.wait()
+        store.start()
+    for store in stores:
+        store.wait()
 
 
 def on_device(residual, out_proj, attn_in, stash_slots, grad_in, stash_slot):
@@ -315,12 +325,20 @@
         ),
         name="tick",
     )(stash_slot, residual, out_proj, attn_in, stash_slots, grad_in)
+    bands = 4
     return pl.pallas_call(
         settle,
         out_shape=results,
         in_specs=[anywhere] * 3,
         out_specs=(anywhere,) * 3,
-        scratch_shapes=[pltpu.SemaphoreType.DMA((3,))],
+        scratch_shapes=[
+            pltpu.VMEM((bands, rows // bands, depth), low),
+            pltpu.VMEM((parts, rows, local), low),
+            pltpu.VMEM((parts, rows, local), low),
+            pltpu.SemaphoreType.DMA((bands + 2 * parts,)),
+            pltpu.SemaphoreType.DMA((bands + 2 * parts,)),
+        ],
+        compiler_params=pltpu.CompilerParams(vmem_limit_bytes=VMEM_LIMIT),
         name="settle",
     )(*made)
 

time: 171 us -> 84.4 us (0.49)
  Pallas kernels: 161 us -> 83.6 us
  local copies, waits for them, and re-layouts: 8.4 us -> 0 us
    pallas_call x1, Pallas kernels: 80.5 us -> 2.6 us  [on_device(): pl.pallas_call(settle, out_shape=results, in_specs=[anywhere] * 3, out_sp...]
    unnamed x16 -> x0, local copies, waits for them, and re-layouts: 8.4 us -> none
where the time goes in v2:
time: 84.4 us; the launch traced here: 84.2 us
  Pallas kernels  83.6 us (99%)
    pallas_call x1, Pallas kernels, on_device(): pl.pallas_call(functools.partial(tick, sections, group), out_shape=result...  81 us
    pallas_call x1, Pallas kernels, on_device(): pl.pallas_call(settle, out_shape=results, in_specs=[anywhere] * 3, out_sp...  2.6 us

profile of v2, /device:TPU:17, one launch (start us, length us, event | category | flops | bytes accessed | tf_op | source)
XLA Modules:
  0.0 84.2 jit_solution(4395705341075697322)
XLA Ops:
  0.6 81.0 %tick.1 = (bf16[1,128,4096]{2,1,0:T(8,128)(2,1)}, bf16[1,3,128,1024]{3,2,1,0:T(8,128)(2,1)}, bf16[1,3,128,1024]{3,2,1,0:T(8,128)(2,1)}) custom-call(s32[8]{0:T(128)} %slot_ref.1, bf16[1,128,4096]{2,1,0:T(8,128)(2,1)} %residual_ref.1, bf16[1,1024,4096]{2,1,0:T(8,128)(2,1)} %weight_ref.1, bf16[1,3,128,1024]{3,2,1,0:T(8,128)(2,1)} %attn_ref.1, ...), custom_call_target="tpu_custom_call" | custom-call | flops 2415919104 | bytes 8388608 | tf_op jit(solution)/shard_map/tick/pallas_call | solution.py:287
  81.6 2.6 %settle.1 = (bf16[1,128,4096]{2,1,0:T(8,128)(2,1)}, bf16[1,3,128,1024]{3,2,1,0:T(8,128)(2,1)}, bf16[1,3,128,1024]{3,2,1,0:T(8,128)(2,1)}) custom-call(bf16[1,128,4096]{2,1,0:T(8,128)(2,1)} %get-tuple-element.6.refs_0_, bf16[1,3,128,1024]{3,2,1,0:T(8,128)(2,1)} %get-tuple-element.7.refs_1_, bf16[1,3,128,1024]{3,2,1,0:T(8,128)(2,1)} %get-tuple-element.8.refs_2_), custom_call_target="tpu_custom_call" | custom-call | tf_op jit(solution)/shard_map/settle/pallas_call | solution.py:329

commit v3 on v2

--- a/solution.py
+++ b/solution.py
@@ -51,34 +51,48 @@
     context,
     grad_context,
     own_sum,
-    sums_out,
-    sums_in,
+    mate_out,
+    mate_in,
+    cross_in,
     piece_out,
     piece_in,
+    relayed,
     qkv,
     local_sem,
     evict_send,
     evict_recv,
     request_send,
     request_recv,
-    sums_send,
-    sums_recv,
+    mate_send,
+    mate_recv,
+    cross_send,
+    cross_recv,
     piece_send,
     piece_recv,
+    relay_send,
+    relay_recv,
     gather_send,
     gather_recv,
+    pass_send,
+    pass_recv,
 ):
     section = lax.axis_index("pipe")
     shard = lax.axis_index("tensor")
     partner = lax.rem(section + sections // 2, sections)
     following = lax.rem(section + 1, sections)
     before = lax.rem(section + sections - 1, sections)
+    two_on = lax.rem(section + 2, sections)
+    two_back = lax.rem(section + sections - 2, sections)
+    odd = lax.rem(section, 2) == 1
+    chips = group // 2
+    chip, core = shard // 2, lax.rem(shard, 2)
+    mate = shard + 1 - 2 * core
     parts, rows, local = attn.shape
     width = piece_out.shape[1]
     heads = local // HD
 
-    def peer(distance):
-        return lax.rem(shard + distance, group)
+    def on_chip(distance, which):
+        return lax.rem(chip + distance, chips) * 2 + which
 
     def lanes(index, size):
         return pl.ds(pl.multiple_of(index * size, size), size)
@@ -98,33 +112,31 @@
         loads.append(load)
 
     barrier = pltpu.get_barrier_semaphore()
-    for other in (partner, following, before):
+    for other in (partner, following, before, two_on, two_back):
         pl.semaphore_signal(barrier, inc=1, device_id=(other, shard), device_id_type=MESH)
-    for distance in range(1, group):
-        pl.semaphore_signal(
-            barrier, inc=1, device_id=(section, peer(distance)), device_id_type=MESH
-        )
-    pl.semaphore_wait(barrier, 3 + group - 1)
+    for other in [mate] + [on_chip(distance, core) for distance in range(1, chips)]:
+        pl.semaphore_signal(barrier, inc=1, device_id=(section, other), device_id_type=MESH)
+    pl.semaphore_wait(barrier, 5 + chips)
+
+    def remote(source, target, send, recv, number, where):
+        return pltpu.make_async_remote_copy(
+            src_ref=source,
+            dst_ref=target,
+            send_sem=send.at[number],
+            recv_sem=recv.at[number],
+            device_id=where,
+            device_id_type=MESH,
+        )
 
     evictions = [
-        pltpu.make_async_remote_copy(
-            src_ref=attn_ref.at[0, part],
-            dst_ref=evict_ref.at[0, part],
-            send_sem=evict_send.at[part],
-            recv_sem=evict_recv.at[part],
-            device_id=(partner, shard),
-            device_id_type=MESH,
+        remote(
+            attn_ref.at[0, part], evict_ref.at[0, part], evict_send, evict_recv, part, (partner, shard)
         )
         for part in range(parts)
     ]
     requests = [
-        pltpu.make_async_remote_copy(
-            src_ref=request.at[part],
-            dst_ref=stored.at[part],
-            send_sem=request_send.at[part],
-            recv_sem=request_recv.at[part],
-            device_id=(partner, shard),
-            device_id_type=MESH,
+        remote(
+            request.at[part], stored.at[part], request_send, request_recv, part, (partner, shard)
         )
         for part in range(parts)
     ]
@@ -134,7 +146,8 @@
     loads[0].wait()
     for part in range(parts):
         request[part] = stash[wanted, part]
-        requests[part].start()
+        if part < parts - 1:
+            requests[part].start()
 
     loads[1].wait()
 
@@ -150,26 +163,46 @@
     lax.fori_loop(0, heads, attend, 0, unroll=2)
 
     loads[2].wait()
-    transfers = []
-    for distance in range(1, group):
-        target = peer(distance)
-        sums_out[distance - 1] = jnp.dot(
-            context[...], weight[:, lanes(target, width)], preferred_element_type=jnp.float32
-        )
-        transfer = pltpu.make_async_remote_copy(
-            src_ref=sums_out.at[distance - 1],
-            dst_ref=sums_in.at[distance - 1],
-            send_sem=sums_send.at[distance - 1],
-            recv_sem=sums_recv.at[distance - 1],
-            device_id=(section, target),
-            device_id_type=MESH,
-        )
-        transfer.start()
-        transfers.append(transfer)
+
+    def branch(piece):
+        return jnp.dot(
+            context[...], weight[:, lanes(piece, width)], preferred_element_type=jnp.float32
+        )
+
+    order = list(range(1, chips)) + [0]
+    mates, crossings = {}, {}
+
+    def give_mate(distance):
+        mate_out[distance] = branch(on_chip(distance, 1 - core))
+        mates[distance] = remote(
+            mate_out.at[distance],
+            mate_in.at[distance],
+            mate_send,
+            mate_recv,
+            distance,
+            (section, mate),
+        )
+        mates[distance].start()
+
+    for distance in order[:-1]:
+        give_mate(distance)
+    for distance in order[:-1]:
+        own_sum[distance] = branch(on_chip(distance, core))
+    give_mate(0)
+    for distance in order[:-1]:
+        mates[distance].wait_recv()
+        own_sum[distance] = own_sum[distance] + mate_in[distance]
+        crossings[distance] = remote(
+            own_sum.at[distance],
+            cross_in.at[distance - 1],
+            cross_send,
+            cross_recv,
+            distance - 1,
+            (section, on_chip(distance, core)),
+        )
+        crossings[distance].start()
     loads[4].wait()
-    own_sum[...] = resid[...].astype(jnp.float32) + jnp.dot(
-        context[...], weight[:, lanes(shard, width)], preferred_element_type=jnp.float32
-    )
+    own_sum[0] = resid[...].astype(jnp.float32) + branch(shard)
 
     loads[3].wait()
     tile = min(local, 2 * HD)
@@ -181,40 +214,68 @@
 
     lax.fori_loop(0, local // tile, back_project, 0)
 
-    for transfer in transfers:
-        transfer.wait()
-    total = own_sum[...]
-    for distance in range(1, group):
-        total = total + sums_in[distance - 1]
+    mates[0].wait_recv()
+    total = own_sum[0] + mate_in[0]
+    for distance in range(1, chips):
+        crossings[distance].wait_recv()
+        total = total + cross_in[distance - 1]
     piece_out[...] = total.astype(jnp.bfloat16)
-    hand_over = pltpu.make_async_remote_copy(
-        src_ref=piece_out,
-        dst_ref=piece_in,
-        send_sem=piece_send.at[0],
-        recv_sem=piece_recv.at[0],
-        device_id=(following, shard),
-        device_id_type=MESH,
-    )
-    hand_over.start()
+
+    half = rows // 2
+    upper, lower = pl.ds(0, half), pl.ds(half, half)
+    direct_upper = remote(
+        piece_out.at[upper], piece_in.at[upper], piece_send, piece_recv, 0, (following, shard)
+    )
+    direct_lower = remote(
+        piece_out.at[lower], piece_in.at[lower], piece_send, piece_recv, 1, (following, shard)
+    )
+    detour = remote(
+        piece_out.at[lower], relayed, relay_send, relay_recv, 0, (before, shard)
+    )
+    onward = remote(
+        relayed, piece_in.at[lower], relay_send, piece_recv, 1, (two_on, shard)
+    )
+    direct_upper.start()
+
+    @pl.when(odd)
+    def _():
+        detour.start()
+
+    @pl.when(jnp.logical_not(odd))
+    def _():
+        direct_lower.start()
+        detour.wait_recv()
+        onward.start()
+
+    requests[parts - 1].start()
     for part in range(1, parts):
         evictions[part].start()
 
-    hand_over.wait()
+    direct_upper.wait_recv()
+    direct_lower.wait_recv()
     own_columns = lanes(shard, width)
-    gathers = []
-    for distance in range(1, group):
-        gather = pltpu.make_async_remote_copy(
-            src_ref=piece_in,
-            dst_ref=fwd_ref.at[0, :, own_columns],
-            send_sem=gather_send.at[distance - 1],
-            recv_sem=gather_recv.at[distance - 1],
-            device_id=(section, peer(distance)),
-            device_id_type=MESH,
+    keep = pltpu.make_async_copy(piece_in, fwd_ref.at[0, :, own_columns], local_sem.at[5])
+    keep.start()
+    gathers, passes = [], []
+    for distance in list(range(1, chips)) + [0]:
+        target = mate if distance == 0 else on_chip(distance, core)
+        gather = remote(
+            piece_in,
+            fwd_ref.at[0, :, own_columns],
+            gather_send,
+            gather_recv,
+            distance,
+            (section, target),
         )
         gather.start()
         gathers.append(gather)
-    keep = pltpu.make_async_copy(piece_in, fwd_ref.at[0, :, own_columns], local_sem.at[5])
-    keep.start()
+    for distance in range(1, chips):
+        gathers[distance - 1].wait_recv()
+        columns = lanes(on_chip(chips - distance, core), width)
+        arrived = fwd_ref.at[0, :, columns]
+        passed = remote(arrived, arrived, pass_send, pass_recv, distance - 1, (section, mate))
+        passed.start()
+        passes.append(passed)
 
     for copy in requests:
         copy.wait()
@@ -241,9 +302,21 @@
 
     keep.wait()
     put.wait()
-    for copy in gathers:
-        copy.wait()
-    for copy in evictions:
+    for copy in list(mates.values()) + list(crossings.values()) + gathers:
+        copy.wait_send()
+    direct_upper.wait_send()
+
+    @pl.when(odd)
+    def _():
+        detour.wait_send()
+
+    @pl.when(jnp.logical_not(odd))
+    def _():
+        direct_lower.wait_send()
+        onward.wait_send()
+
+    gathers[-1].wait_recv()
+    for copy in passes + evictions:
         copy.wait()
 
 
@@ -276,6 +349,7 @@
     slots = stash_slots.shape[1]
     depth = residual.shape[2]
     width = depth // group
+    chips = group // 2
     anywhere = pl.BlockSpec(memory_space=pl.ANY)
     results = (
         jax.ShapeDtypeStruct((1, rows, depth), jnp.bfloat16),
@@ -299,23 +373,31 @@
             pltpu.VMEM((parts, rows, local), low),
             pltpu.VMEM((rows, local), low),
             pltpu.VMEM((rows, local), low),
-            pltpu.VMEM((rows, width), full),
-            pltpu.VMEM((group - 1, rows, width), full),
-            pltpu.VMEM((group - 1, rows, width), full),
+            pltpu.VMEM((chips, rows, width), full),
+            pltpu.VMEM((chips, rows, width), full),
+            pltpu.VMEM((chips, rows, width), full),
+            pltpu.VMEM((chips - 1, rows, width), full),
             pltpu.VMEM((rows, width), low),
             pltpu.VMEM((rows, width), low),
+            pltpu.VMEM((rows // 2, width), low),
             pltpu.VMEM((parts, rows, local), low),
             pltpu.SemaphoreType.DMA((7,)),
             pltpu.SemaphoreType.DMA((parts,)),
             pltpu.SemaphoreType.DMA((parts,)),
             pltpu.SemaphoreType.DMA((parts,)),
             pltpu.SemaphoreType.DMA((parts,)),
-            pltpu.SemaphoreType.DMA((group - 1,)),
-            pltpu.SemaphoreType.DMA((group - 1,)),
+            pltpu.SemaphoreType.DMA((chips,)),
+            pltpu.SemaphoreType.DMA((chips,)),
+            pltpu.SemaphoreType.DMA((chips - 1,)),
+            pltpu.SemaphoreType.DMA((chips - 1,)),
+            pltpu.SemaphoreType.DMA((2,)),
+            pltpu.SemaphoreType.DMA((2,)),
+            pltpu.SemaphoreType.DMA((2,)),
             pltpu.SemaphoreType.DMA((1,)),
-            pltpu.SemaphoreType.DMA((1,)),
-            pltpu.SemaphoreType.DMA((group - 1,)),
-            pltpu.SemaphoreType.DMA((group - 1,)),
+            pltpu.SemaphoreType.DMA((chips,)),
+            pltpu.SemaphoreType.DMA((chips,)),
+            pltpu.SemaphoreType.DMA((chips - 1,)),
+            pltpu.SemaphoreType.DMA((chips - 1,)),
         ],
         compiler_params=pltpu.CompilerParams(
             collective_id=0, has_side_effects=True, vmem_limit_bytes=VMEM_LIMIT

time: 84.4 us -> 81 us (0.960)
  the two profiles are of different devices: /device:TPU:17 before, /device:TPU:0 now
where the time goes in v3:
time: 81 us; the launch traced here: 80.8 us
  Pallas kernels  80.2 us (99%)
    pallas_call x1, Pallas kernels, on_device(): pl.pallas_call(functools.partial(tick, sections, group), out_shape=result...  77.6 us
    pallas_call x1, Pallas kernels, on_device(): pl.pallas_call(settle, out_shape=results, in_specs=[anywhere] * 3, out_sp...  2.6 us

profile of v3, /device:TPU:0, one launch (start us, length us, event | category | flops | bytes accessed | tf_op | source)
XLA Modules:
  0.0 80.8 jit_solution(5589442943858907630)
XLA Ops:
  0.6 77.6 %tick.1 = (bf16[1,128,4096]{2,1,0:T(8,128)(2,1)}, bf16[1,3,128,1024]{3,2,1,0:T(8,128)(2,1)}, bf16[1,3,128,1024]{3,2,1,0:T(8,128)(2,1)}) custom-call(s32[8]{0:T(128)} %slot_ref.1, bf16[1,128,4096]{2,1,0:T(8,128)(2,1)} %residual_ref.1, bf16[1,1024,4096]{2,1,0:T(8,128)(2,1)} %weight_ref.1, bf16[1,3,128,1024]{3,2,1,0:T(8,128)(2,1)} %attn_ref.1, ...), custom_call_target="tpu_custom_call" | custom-call | flops 2415919104 | bytes 8388608 | tf_op jit(solution)/shard_map/tick/pallas_call | solution.py:361
  78.2 2.6 %settle.1 = (bf16[1,128,4096]{2,1,0:T(8,128)(2,1)}, bf16[1,3,128,1024]{3,2,1,0:T(8,128)(2,1)}, bf16[1,3,128,1024]{3,2,1,0:T(8,128)(2,1)}) custom-call(bf16[1,128,4096]{2,1,0:T(8,128)(2,1)} %get-tuple-element.6.refs_0_, bf16[1,3,128,1024]{3,2,1,0:T(8,128)(2,1)} %get-tuple-element.7.refs_1_, bf16[1,3,128,1024]{3,2,1,0:T(8,128)(2,1)} %get-tuple-element.8.refs_2_), custom_call_target="tpu_custom_call" | custom-call | tf_op jit(solution)/shard_map/settle/pallas_call | solution.py:411
